TPU v7x, 768 devices: a whole 4x8x12 slice. The times are simulated.
768 devices in a mesh: blk: 128 (over z_hi, y, x, core), group: 6 (over z_lo).
Axes of the slice: x: 4, y: 8, z: 12 (z_hi: 2, z_lo: 6; z = z_hi * 6 + z_lo), core: 2. Of those that a mesh axis runs over, the one named last changes fastest.
Arguments:
- aggregated_vision_descriptors: bfloat16 [98304, 1152], P(('blk', 'group')), may hold values from -24 to 24
- caption_vectors_unnormed: bfloat16 [98304, 1152], P(('blk', 'group')), may hold values from -0.19921875 to 0.19921875
- vision_projection_coefficients: bfloat16 [1152, 1152], replicated, may hold values from -0.1875 to 0.1875
- score_multiplier: float32 [1], replicated, may hold values from 5 to 15
- score_shift_term: float32 [1], replicated, may hold values from -3 to -1
Outputs:
- head_grad: bfloat16 [1152, 1152], P('blk')
- text_grad: bfloat16 [98304, 1152], P(('blk', 'group'))
All inputs are finite; a program needn't handle non-finite values.
Results may differ from a plain program's by a relative error of at most 0.0095.
Values may be sent and summed in bfloat16 or wider, within the bound.
A program may use at most 32 MiB of HBM per device.

v0:
```python
import jax
import jax.numpy as jnp
from jax import lax
from jax.sharding import PartitionSpec as P

epsilon = 1e-06


def shifted(block, axis, distance):
    devices = range(lax.axis_size(axis))
    route = [((i - distance) % len(devices), i) for i in devices]
    return lax.ppermute(block, axis, route)


def cycle_step(text_block, text_accum):
    moved_block = shifted(text_block, "blk", 1)
    moved_accum = shifted(text_accum, "blk", 1)
    return (moved_block, moved_accum)


def local(
    aggregated_vision_descriptors,
    caption_vectors_unnormed,
    vision_projection_coefficients,
    score_multiplier,
    score_shift_term,
):
    row_count = aggregated_vision_descriptors.shape[0]
    width = aggregated_vision_descriptors.shape[1]
    projected = jnp.dot(
        aggregated_vision_descriptors,
        vision_projection_coefficients,
        preferred_element_type=jnp.float32,
    )
    img_inverse = lax.rsqrt(jnp.sum(projected * projected, axis=1, keepdims=True) + epsilon)
    unit_img = projected * img_inverse
    img_b = unit_img.astype(jnp.bfloat16)
    multiplier_scalar = score_multiplier[0]
    bias_value = score_shift_term[0]
    positive = jnp.eye(row_count, dtype=jnp.float32)

    def visit_block(text_block, text_accum, image_grad, is_own):
        text_wide = text_block.astype(jnp.float32)
        txt_inverse = lax.rsqrt(jnp.sum(text_wide * text_wide, axis=1, keepdims=True) + epsilon)
        txt_b = (text_wide * txt_inverse).astype(jnp.bfloat16)
        match_scores = (
            multiplier_scalar
            * lax.dot_general(
                img_b, txt_b, (((1,), (1,)), ((), ())), preferred_element_type=jnp.float32
            )
            + bias_value
        )
        projection_coefficients = jax.nn.sigmoid(match_scores)
        if is_own:
            projection_coefficients = projection_coefficients - positive
        stretched_scores = (multiplier_scalar * projection_coefficients).astype(jnp.bfloat16)
        image_grad = image_grad + jnp.dot(
            stretched_scores, txt_b, preferred_element_type=jnp.float32
        )
        text_accum = text_accum + lax.dot_general(
            stretched_scores, img_b, (((0,), (0,)), ((), ())), preferred_element_type=jnp.float32
        )
        return (text_accum, image_grad)

    text_block = caption_vectors_unnormed
    text_accum = jnp.zeros((row_count, width), jnp.float32)
    image_grad = jnp.zeros((row_count, width), jnp.float32)
    text_accum, image_grad = visit_block(text_block, text_accum, image_grad, True)
    text_block, text_accum = cycle_step(text_block, text_accum)
    text_accum, image_grad = visit_block(text_block, text_accum, image_grad, False)
    text_block = shifted(text_block, "group", 1)
    text_accum = shifted(text_accum.astype(jnp.bfloat16), "group", 1).astype(text_accum.dtype)
    text_accum, image_grad = visit_block(text_block, text_accum, image_grad, False)
    text_block, text_accum = cycle_step(text_block, text_accum)
    text_accum, image_grad = visit_block(text_block, text_accum, image_grad, False)
    final_wide = text_block.astype(jnp.float32)
    txt_inverse = lax.rsqrt(jnp.sum(final_wide * final_wide, axis=1, keepdims=True) + epsilon)
    unit_txt = final_wide * txt_inverse
    text_grad = (
        (text_accum - unit_txt * jnp.sum(unit_txt * text_accum, axis=1, keepdims=True))
        * txt_inverse
    ).astype(jnp.bfloat16)
    proj_grad = (
        (image_grad - unit_img * jnp.sum(unit_img * image_grad, axis=1, keepdims=True))
        * img_inverse
    ).astype(jnp.bfloat16)
    column_span = width // lax.axis_size("group")
    column_start = lax.axis_index("group") * column_span
    all_factors = (
        lax.all_gather(aggregated_vision_descriptors, "group", axis=0, tiled=True),
        lax.all_gather(proj_grad, "group", axis=0, tiled=True),
    )
    my_columns = lax.dynamic_slice_in_dim(all_factors[1], column_start, column_span, 1)
    left_part = all_factors[0]
    shard_sum = lax.psum_scatter(
        lax.dot_general(
            left_part, my_columns, (((0,), (0,)), ((), ())), preferred_element_type=jnp.float32
        ),
        "blk",
        scatter_dimension=0,
        tiled=True,
    )
    head_sum = lax.all_gather(shard_sum, "group", axis=1, tiled=True)
    return (head_sum.astype(jnp.bfloat16), text_grad)


def solution(mesh):
    in_specs = (P(("blk", "group"), None), P(("blk", "group"), None), P(), P(), P())
    out_specs = (P("blk", None), P(("blk", "group"), None))
    return jax.shard_map(local, mesh=mesh, in_specs=in_specs, out_specs=out_specs, check_vma=False)
```

profile of v0, /device:TPU:1, one launch (start us, length us, event | category | flops | bytes accessed | tf_op | source)
XLA Modules:
  0.0 1168.4 jit_solution(12819363910448303783)
XLA Ops:
  7.2 0.0 copy-start
  7.2 0.0 all-gather.6.cloned.1.call-start
  7.2 4.6 collective-permute-start
  11.9 0.0 all-gather.6.cloned.1.call-update
  11.9 0.0 all-gather.4.cloned.1.call-start
  11.9 1.1 fusion.33
  13.1 0.0 copy-done
  13.1 0.0 copy-start.1
  13.1 1.7 multiply_reduce_fusion.1
  16.1 0.1 multiply_convert_fusion.1
  16.2 0.0 copy-done.1
  16.2 0.3 fusion.26
  16.6 1.1 fusion.55
  17.6 1.9 collective-permute-start.3
  19.6 0.3 fusion.49
  19.9 1.2 collective-permute-done
  21.1 0.1 fusion.35
  21.2 2.8 collective-permute-start.1
  24.0 0.3 fusion.27
  24.4 0.3 convolution_add_fusion.3
  24.7 11.9 %collective-permute-done.1 = bf16[128,1152]{1,0:T(8,128)(2,1)S(1)} collective-permute-done((bf16[128,1152]{1,0:T(8,128)(2,1)S(1)}, bf16[128,1152]{1,0:T(8,128)(2,1)S(1)}, u32[]{:S(2)}, u32[]{:S(2)}) %collective-permute-start.1) | collective-permute-done | bytes 294944 | tf_op jit(solution)/shard_map/ppermute | solution.py:12
  36.6 7.0 collective-permute-start.2
  43.5 0.1 fusion.37
  43.7 0.3 fusion.28
  44.0 0.3 convolution_add_fusion.2
  44.4 15.3 %collective-permute-done.2 = bf16[128,1152]{1,0:T(8,128)(2,1)S(1)} collective-permute-done((bf16[128,1152]{1,0:T(8,128)(2,1)S(1)}, bf16[128,1152]{1,0:T(8,128)(2,1)S(1)}, u32[]{:S(2)}, u32[]{:S(2)}) %collective-permute-start.2) | collective-permute-done | bytes 294944 | tf_op jit(solution)/shard_map/ppermute | solution.py:12
  59.6 0.1 fusion.43
  59.8 0.4 fusion.29
  60.1 0.4 multiply_reduce_fusion
  60.5 0.9 multiply_convert_fusion
  61.4 0.0 all-gather.4.cloned.1.call-update
  61.5 0.0 collective-permute-done.3
  61.5 1.3 fusion
  62.8 1.9 collective-permute-start.4
  64.7 0.3 fusion.56
  65.0 17.2 %collective-permute-done.4 = bf16[128,1152]{1,0:T(8,128)(2,1)S(1)} collective-permute-done((bf16[128,1152]{1,0:T(8,128)(2,1)S(1)}, bf16[128,1152]{1,0:T(8,128)(2,1)S(1)}, u32[]{:S(2)}, u32[]{:S(2)}) %collective-permute-start.4) | collective-permute-done | bytes 294944 | tf_op jit(solution)/shard_map/ppermute | solution.py:12
  82.2 0.9 convert_add_fusion
  83.0 1.9 collective-permute-start.5
  85.0 1.3 dynamic-slice
  86.9 0.3 fusion.57
  87.2 41.8 %collective-permute-done.5 = f32[128,1152]{1,0:T(8,128)} collective-permute-done((f32[128,1152]{1,0:T(8,128)}, f32[128,1152]{1,0:T(8,128)}, u32[]{:S(2)}, u32[]{:S(2)}) %collective-permute-start.5) | collective-permute-done | bytes 589856 | tf_op jit(solution)/shard_map/ppermute | solution.py:12
  128.9 1.3 fusion.39
  130.2 0.9 fusion.42
  131.1 0.0 all-gather.6.cloned.1.call-done
  131.1 29.1 %all-gather.4.cloned.1.call-done = bf16[768,1152]{1,0:T(8,128)(2,1)} async-done(((bf16[128,1152]{1,0:T(8,128)(2,1)}), bf16[768,1152]{1,0:T(8,128)(2,1)}) %all-gather.4.cloned.1.call-update) | async-done | bytes 1769488 | tf_op jit(solution)/shard_map/all_gather | solution.py:91
  160.2 2.3 convolution_bitcast_fusion
  162.6 972.2 %all-reduce.2 = bf16[1152,192]{0,1:T(8,128)(2,1)} all-reduce(f32[1152,192]{0,1:T(8,128)S(1)} %convolution_bitcast_fusion), channel_id=2, replica_groups=mesh['blk'=128,'group'=6] {'blk'}, use_global_device_ids=true, to_apply=%region_6.0.clone | all-reduce | flops 221184 | bytes 1327104
  1134.8 1.0 dynamic-slice_bitcast_fusion
  1135.7 0.1 copy.11
  1135.8 25.0 %all-gather = bf16[6,192,9]{1,2,0:T(8,128)(2,1)S(1)} all-gather(bf16[1,192,9]{1,2,0:T(8,128)(2,1)S(1)} %copy.11), channel_id=1, replica_groups=mesh['blk'=128,'group'=6] {'group'}, dimensions={0}, use_global_device_ids=true | all-gather | bytes 24192 | tf_op jit(solution)/shard_map/all_gather | solution.py:103
  1160.9 0.7 reshape.38
  (6 shorter events, 0.0 us)
Async XLA Ops:
  7.2 5.9 copy-start
  7.2 124.0 %all-gather.6.cloned.1.call-start = ((), (), s32[]{:S(2)}) async-start(), calls=%async_computation.1 | async-start | bytes 2064384 | tf_op jit(solution)/shard_map/all_gather | solution.py:90
  7.2 13.8 %collective-permute-start = (bf16[128,1152]{1,0:T(8,128)(2,1)}, bf16[128,1152]{1,0:T(8,128)(2,1)S(1)}, u32[]{:S(2)}, u32[]{:S(2)}) collective-permute-start(bf16[128,1152]{1,0:T(8,128)(2,1)} %param.6), channel_id=1, source_target_pairs={{762,0},{0,6},{6,12},{12,18},{18,24},{24,30},{30,36},{36,42},{42,4... | collective-permute-start | bytes 884744 | tf_op jit(solution)/shard_map/ppermute | solution.py:12
  11.9 148.3 %all-gather.4.cloned.1.call-start = ((), (), s32[]{:S(2)}) async-start(), calls=%async_computation | async-start | bytes 2064384 | tf_op jit(solution)/shard_map/all_gather | solution.py:91
  13.1 3.1 copy-start.1
  17.6 43.8 %collective-permute-start.3 = (f32[128,1152]{1,0:T(8,128)}, f32[128,1152]{1,0:T(8,128)}, u32[]{:S(2)}, u32[]{:S(2)}) collective-permute-start(f32[128,1152]{1,0:T(8,128)} %fusion.55), channel_id=1, source_target_pairs={{762,0},{0,6},{6,12},{12,18},{18,24},{24,30},{30,36},{36,42},{42,4... | collective-permute-start | bytes 1769480 | tf_op jit(solution)/shard_map/ppermute | solution.py:12
  21.2 15.4 %collective-permute-start.1 = (bf16[128,1152]{1,0:T(8,128)(2,1)S(1)}, bf16[128,1152]{1,0:T(8,128)(2,1)S(1)}, u32[]{:S(2)}, u32[]{:S(2)}) collective-permute-start(bf16[128,1152]{1,0:T(8,128)(2,1)S(1)} %collective-permute-done), channel_id=1, source_target_pairs={{5,0},{0,1},{1,2},{2,3},{3,4},{4,5},{11,6},{6,7},{7,8},{8,9},{9,10... | collective-permute-start | bytes 884744 | tf_op jit(solution)/shard_map/ppermute | solution.py:12
  36.6 23.0 %collective-permute-start.2 = (bf16[128,1152]{1,0:T(8,128)(2,1)S(1)}, bf16[128,1152]{1,0:T(8,128)(2,1)S(1)}, u32[]{:S(2)}, u32[]{:S(2)}) collective-permute-start(bf16[128,1152]{1,0:T(8,128)(2,1)S(1)} %collective-permute-done.1), channel_id=1, source_target_pairs={{762,0},{0,6},{6,12},{12,18},{18,24},{24,30},{30,36},{36,42},{42,4... | collective-permute-start | bytes 884744 | tf_op jit(solution)/shard_map/ppermute | solution.py:12
  62.8 19.4 %collective-permute-start.4 = (bf16[128,1152]{1,0:T(8,128)(2,1)S(1)}, bf16[128,1152]{1,0:T(8,128)(2,1)S(1)}, u32[]{:S(2)}, u32[]{:S(2)}) collective-permute-start(bf16[128,1152]{1,0:T(8,128)(2,1)S(1)} %fusion), channel_id=1, source_target_pairs={{5,0},{0,1},{1,2},{2,3},{3,4},{4,5},{11,6},{6,7},{7,8},{8,9},{9,10... | collective-permute-start | bytes 884744 | tf_op jit(solution)/shard_map/ppermute | solution.py:12
  83.0 45.9 %collective-permute-start.5 = (f32[128,1152]{1,0:T(8,128)}, f32[128,1152]{1,0:T(8,128)}, u32[]{:S(2)}, u32[]{:S(2)}) collective-permute-start(f32[128,1152]{1,0:T(8,128)} %convert_add_fusion), channel_id=1, source_target_pairs={{762,0},{0,6},{6,12},{12,18},{18,24},{24,30},{30,36},{36,42},{42,4... | collective-permute-start | bytes 1769480 | tf_op jit(solution)/shard_map/ppermute | solution.py:12
Sparse Core Ops, SparseCore 0:
  12.0 66.2 all-gather.5
  80.7 79.4 all-gather.3
where the time goes:
time: 1180 us; the launch traced here: 1170 us
  blocking collectives  997 us (84%)
  waiting for transfers between devices  116 us (10%)
  starting transfers between devices  20.2 us (2%)
  between operations  16.2 us (1%)
    unnamed x1, blocking collectives  972 us
    ppermute x6, waiting for transfers between devices, shifted(): return lax.ppermute(block, axis, route)  87.2 us
    all_gather x1, waiting for transfers between devices, local(): lax.all_gather(proj_grad, 'group', axis=0, tiled=True)  29.1 us
    all_gather x1, blocking collectives, local(): head_sum = lax.all_gather(shard_sum, 'group', axis=1, tiled=True)  25 us
  transfers between devices with their start and end apart: 8, of which 6 were waited for; matrix products, arithmetic and copies ran while one was open for 1% of the time, Pallas kernels for 0%

commit v1 on v0

v1 whole, which is shorter than its diff:
```python
import jax
import jax.numpy as jnp
import numpy as np
from jax import lax
from jax.experimental import pallas as pl
from jax.experimental.pallas import tpu as pltpu
from jax.sharding import PartitionSpec as P

MESH = pl.DeviceIdType.MESH
EPS = 1e-06
NC, NX, NY, NZ, NG = 2, 4, 8, 12, 6
ROWS, D = 128, 1152
NT = D // 128
OWN = 9
BLOCK = 144
PIECE = 96
CHUNKS = 2
F32, BF16 = jnp.float32, jnp.bfloat16


def dot(a, b, ca=1, cb=0):
    return lax.dot_general(a, b, (((ca,), (cb,)), ((), ())), preferred_element_type=F32)


def unit_rows(wide):
    inverse = lax.rsqrt(jnp.sum(wide * wide, axis=1, keepdims=True) + EPS)
    return wide * inverse, inverse


def kernel(
    mult_ref, bias_ref, a_ref, t_ref, w_hbm, order_hbm,
    head_ref, tgrad_ref,
    w_ref, order_ref, proj_ref, img_ref, tx, ix, igrad, tsum,
    at_all, at_got, p_got, out, pieces, ysend, ygot, ysum, zsend, zgot, final,
    local_sem, t_ss, t_rs, i_ss, i_rs, a_ss, a_rs, p_ss, p_rs, q_ss, q_rs, y_ss, y_rs, z_ss, z_rs,
):
    b = lax.axis_index("blk")
    g = lax.axis_index("group")
    c, x, y, zh = b % 2, (b // 2) % NX, (b // 8) % NY, b // 64
    z = zh * NG + g

    def at(c_, x_, y_, z_):
        return ((z_ // NG) * 64 + y_ * 8 + x_ * 2 + c_, z_ % NG)

    after = ((b + 1) % 128, g)
    before = ((b + 127) % 128, g)
    up = (b, (g + 1) % NG)
    down = (b, (g + 5) % NG)
    partner = at(1 - c, x, y, z)

    load_w = pltpu.make_async_copy(w_hbm, w_ref, local_sem.at[0])
    load_w.start()
    load_order = pltpu.make_async_copy(order_hbm, order_ref, local_sem.at[1])
    load_order.start()

    ring = [at(core, (x + k) % NX, y, z) for k in range(1, NX) for core in range(NC)]
    column = [at(c, x, (y + k) % NY, z) for k in range(1, NY)]
    tower = [at(c, x, y, (z + k) % NZ) for k in range(1, NZ)]
    greeted = [after, before, up, down, partner] + ring + column + tower
    barrier = pltpu.get_barrier_semaphore()
    for device in greeted:
        pl.semaphore_signal(barrier, inc=1, device_id=device, device_id_type=MESH)
    pl.semaphore_wait(barrier, len(greeted))

    started = []

    def send(src, dst, ss, rs, device):
        copy = pltpu.make_async_remote_copy(
            src_ref=src, dst_ref=dst, send_sem=ss, recv_sem=rs, device_id=device, device_id_type=MESH
        )
        copy.start()
        started.append(copy)
        return copy

    def chunk(k):
        return pl.ds(k * (ROWS // CHUNKS), ROWS // CHUNKS)

    hop1 = [
        send(t_ref.at[chunk(k)], tx.at[0, chunk(k)], t_ss.at[0, k], t_rs.at[0, k], after)
        for k in range(CHUNKS)
    ]

    multiplier = mult_ref[0]
    bias = bias_ref[0]

    load_w.wait()
    for k in range(3):
        cols = pl.ds(k * 384, 384)
        proj_ref[:, cols] = dot(a_ref[...], w_ref[:, cols])
    unit, img_inverse = unit_rows(proj_ref[...])
    img_ref[...] = unit.astype(BF16)

    load_order.wait()
    for k in range(NX * NC):
        at_all[k] = dot(order_ref[pl.ds(k * BLOCK, BLOCK), :], a_ref[...], 1, 1).astype(BF16)
    at_got[0] = at_all[x * 2 + c]
    a_copies = []
    for k in range(NX):
        for dc in range(NC):
            slot = k * 2 + dc
            if slot == 0:
                continue
            tx_x, tx_c = (x + k) % NX, (c + dc) % 2
            a_copies.append(
                send(
                    at_all.at[tx_x * 2 + tx_c], at_got.at[slot], a_ss.at[slot], a_rs.at[slot],
                    at(tx_c, tx_x, y, z),
                )
            )

    def txt_of(raw):
        return unit_rows(raw.astype(F32))[0].astype(BF16)

    rows = lax.broadcasted_iota(jnp.int32, (ROWS, ROWS), 0)
    cols = lax.broadcasted_iota(jnp.int32, (ROWS, ROWS), 1)
    positive = jnp.where(rows == cols, 1.0, 0.0).astype(F32)

    def scaled_of(left, right, own):
        logits = multiplier * dot(left, right, 1, 1) + bias
        weight = jax.nn.sigmoid(logits)
        if own:
            weight = weight - positive
        return (multiplier * weight).astype(BF16)

    def image_pair(raw, own):
        txt_b = txt_of(raw)
        term = dot(scaled_of(img_ref[...], txt_b, own), txt_b)
        if own:
            igrad[...] = term
        else:
            igrad[...] += term

    hop2 = []
    for k in range(CHUNKS):
        hop1[k].wait_recv()
        hop2.append(send(tx.at[0, chunk(k)], tx.at[1, chunk(k)], t_ss.at[1, k], t_rs.at[1, k], up))
    image_pair(t_ref[...], True)
    image_pair(tx[0], False)
    hop3 = []
    for k in range(CHUNKS):
        hop2[k].wait_recv()
        hop3.append(send(tx.at[1, chunk(k)], tx.at[2, chunk(k)], t_ss.at[2, k], t_rs.at[2, k], after))
    image_pair(tx[1], False)
    for k in range(CHUNKS):
        hop3[k].wait_recv()
    image_pair(tx[2], False)

    unit, img_inverse = unit_rows(proj_ref[...])
    grad = igrad[...]
    p_got[0] = (
        (grad - unit * jnp.sum(unit * grad, axis=1, keepdims=True)) * img_inverse
    ).astype(BF16)

    p_copies = {}
    for k in (2, 1, 3):
        p_copies[k] = send(
            p_got.at[0], p_got.at[k * 2], p_ss.at[k], p_rs.at[k], at(c, (x + k) % NX, y, z)
        )
    q_copies = {0: send(p_got.at[0], p_got.at[1], q_ss.at[0], q_rs.at[0], partner)}
    i_hop1 = send(img_ref, ix.at[0], i_ss.at[0], i_rs.at[0], after)

    for copy in a_copies:
        copy.wait_recv()
    out[...] = dot(at_got[0], p_got[0])
    for k in (1, 3, 2):
        p_copies[k].wait_recv()
        q_copies[k] = send(p_got.at[k * 2], p_got.at[k * 2 + 1], q_ss.at[k], q_rs.at[k], partner)
        out[...] += dot(at_got[k * 2], p_got[k * 2])
    for k in (0, 1, 3, 2):
        q_copies[k].wait_recv()
        out[...] += dot(at_got[k * 2 + 1], p_got[k * 2 + 1])

    for q in range(NY):
        for half in range(2):
            for j in range(NT):
                source = (q * 2 + half) * OWN
                target = half * PIECE + j * OWN
                pieces[q, target : target + OWN, :] = out[source : source + OWN, j * 128 : (j + 1) * 128]
            pad = half * PIECE + NT * OWN
            pieces[q, pad : (half + 1) * PIECE, :] = jnp.zeros((PIECE - NT * OWN, 128), F32)
    ysend[...] = pieces[...].astype(BF16)
    y_copies = []
    for k in (4, 3, 5, 2, 6, 1, 7):
        to_y = (y + k) % NY
        y_copies.append(send(ysend.at[to_y], ygot.at[k], y_ss.at[k], y_rs.at[k], at(c, x, to_y, z)))

    i_hop1.wait_recv()
    i_hop2 = send(ix.at[0], ix.at[1], i_ss.at[1], i_rs.at[1], up)

    total = pieces[y]
    for k, copy in zip((4, 3, 5, 2, 6, 1, 7), y_copies):
        copy.wait_recv()
        total = total + ygot[k].astype(F32)
    zsend[0] = total[:PIECE].astype(BF16)
    zsend[1] = total[PIECE:].astype(BF16)
    zgot[z] = zsend[zh]
    z_copies = []
    for k in (6, 5, 7, 4, 8, 3, 9, 2, 10, 1, 11):
        to_z = (z + k) % NZ
        z_copies.append(
            send(zsend.at[to_z // NG], zgot.at[z], z_ss.at[k], z_rs.at[k], at(c, x, y, to_z))
        )

    i_hop2.wait_recv()
    i_hop3 = send(ix.at[1], ix.at[2], i_ss.at[2], i_rs.at[2], after)

    unit_txt, txt_inverse = unit_rows(tx[2].astype(F32))
    txt_b = unit_txt.astype(BF16)

    def text_pair(image, own):
        return dot(scaled_of(txt_b, image, own), image)

    tsum[...] = text_pair(img_ref[...], False)
    tsum[...] += text_pair(ix[0], False)
    tsum[...] += text_pair(ix[1], False)

    for k, copy in zip((6, 5, 7, 4, 8, 3, 9, 2, 10, 1, 11), z_copies):
        copy.wait_recv()
    total = zgot[0].astype(F32)
    for k in range(1, NZ):
        total = total + zgot[k].astype(F32)
    final[...] = total
    for j in range(NT):
        head_ref[:, j * 128 : (j + 1) * 128] = final[j * OWN : (j + 1) * OWN, :].astype(BF16)

    i_hop3.wait_recv()
    tsum[...] += text_pair(ix[2], True)
    grad = tsum[...]
    unit_txt, txt_inverse = unit_rows(tx[2].astype(F32))
    tgrad_ref[...] = (
        (grad - unit_txt * jnp.sum(unit_txt * grad, axis=1, keepdims=True)) * txt_inverse
    ).astype(BF16)

    for copy in started:
        copy.wait_send()


def row_order():
    source = np.arange(D).reshape(2, NY, NX, NC, OWN).transpose(2, 3, 1, 0, 4).reshape(-1)
    order = np.zeros((D, D), np.float32)
    order[np.arange(D), source] = 1.0
    return order


def local(descriptors, captions, weights, multiplier, bias):
    order = jnp.asarray(row_order(), BF16)
    vmem = pl.BlockSpec(memory_space=pltpu.VMEM)
    smem = pl.BlockSpec(memory_space=pltpu.SMEM)
    hbm = pl.BlockSpec(memory_space=pl.ANY)
    dma = pltpu.SemaphoreType.DMA
    head, text = pl.pallas_call(
        kernel,
        out_shape=(
            jax.ShapeDtypeStruct((OWN, D), BF16),
            jax.ShapeDtypeStruct((ROWS, D), BF16),
        ),
        in_specs=[smem, smem, vmem, vmem, hbm, hbm],
        out_specs=(vmem, vmem),
        scratch_shapes=[
            pltpu.VMEM((D, D), BF16),
            pltpu.VMEM((D, D), BF16),
            pltpu.VMEM((ROWS, D), F32),
            pltpu.VMEM((ROWS, D), BF16),
            pltpu.VMEM((3, ROWS, D), BF16),
            pltpu.VMEM((3, ROWS, D), BF16),
            pltpu.VMEM((ROWS, D), F32),
            pltpu.VMEM((ROWS, D), F32),
            pltpu.VMEM((NX * NC, BLOCK, ROWS), BF16),
            pltpu.VMEM((NX * NC, BLOCK, ROWS), BF16),
            pltpu.VMEM((NX * NC, ROWS, D), BF16),
            pltpu.VMEM((BLOCK, D), F32),
            pltpu.VMEM((NY, 2 * PIECE, 128), F32),
            pltpu.VMEM((NY, 2 * PIECE, 128), BF16),
            pltpu.VMEM((NY, 2 * PIECE, 128), BF16),
            pltpu.VMEM((2 * PIECE, 128), F32),
            pltpu.VMEM((2, PIECE, 128), BF16),
            pltpu.VMEM((NZ, PIECE, 128), BF16),
            pltpu.VMEM((PIECE, 128), F32),
            dma((2,)),
            dma((3, CHUNKS)),
            dma((3, CHUNKS)),
            dma((3,)),
            dma((3,)),
            dma((NX * NC,)),
            dma((NX * NC,)),
            dma((NX,)),
            dma((NX,)),
            dma((NX,)),
            dma((NX,)),
            dma((NY,)),
            dma((NY,)),
            dma((NZ,)),
            dma((NZ,)),
        ],
        compiler_params=pltpu.CompilerParams(
            collective_id=0, has_side_effects=True, vmem_limit_bytes=48 * 1024 * 1024
        ),
        name="window_grads",
    )(multiplier, bias, descriptors, captions, weights, order)
    return head, text


def solution(mesh):
    in_specs = (P(("blk", "group"), None), P(("blk", "group"), None), P(), P(), P())
    out_specs = (P("blk", None), P(("blk", "group"), None))
    return jax.shard_map(local, mesh=mesh, in_specs=in_specs, out_specs=out_specs, check_vma=False)
```

time: 1180 us -> 103 us (0.09)
  the two profiles are of different devices: /device:TPU:1 before, /device:TPU:64 now
where the time goes in v1:
time: 103 us
  Pallas kernels  96.1 us (93%)
  local copies, waits for them, and re-layouts  5 us (5%)
  between operations  1.94 us (2%)
    pallas_call x1, Pallas kernels, local(): pl.pallas_call(kernel, out_shape=(jax.ShapeDtypeStruct((OWN, D), BF16), j...  96.1 us
    unnamed x8, local copies, waits for them, and re-layouts  5 us

profile of v1, /device:TPU:64, one launch (start us, length us, event | category | flops | bytes accessed | tf_op | source)
XLA Modules:
  0.0 103.1 jit_solution(16097183800918280096)
XLA Ops:
  1.9 0.0 copy-start
  1.9 1.7 %copy-done = bf16[1152,1152]{1,0:T(8,128)(2,1)S(1)} copy-done((bf16[1152,1152]{1,0:T(8,128)(2,1)S(1)}, bf16[1152,1152]{1,0:T(8,128)(2,1)}, u32[]{:S(2)}) %copy-start) | copy-done | bytes 2654232
  3.7 0.0 copy-start.1
  3.7 1.0 copy-done.1
  4.6 0.0 copy-start.2
  4.6 1.0 copy-done.2
  5.6 96.1 %window_grads.1 = (bf16[9,1152]{1,0:T(8,128)(2,1)S(1)}, bf16[128,1152]{1,0:T(8,128)(2,1)S(1)}) custom-call(f32[1]{0:T(128)S(6)} %copy.10.mult_ref, f32[1]{0:T(128)S(6)} %copy.11.bias_ref, bf16[128,1152]{1,0:T(8,128)(2,1)S(1)} %copy-done.1, bf16[128,1152]{1,0:T(8,128)(2,1)S(1)} %copy-done.2, bf16[1152,1152]{1,0:T(8,128)(2,1)S(1)} %copy-done, ...), custom_call_target="tpu_custom_call" | custom-call | tf_op jit(solution)/shard_map/window_grads/pallas_call | solution.py:251
  101.7 0.6 copy.12
  102.4 0.7 copy.13
Async XLA Ops:
  1.9 1.8 %copy-start = (bf16[1152,1152]{1,0:T(8,128)(2,1)S(1)}, bf16[1152,1152]{1,0:T(8,128)(2,1)}, u32[]{:S(2)}) copy-start(bf16[1152,1152]{1,0:T(8,128)(2,1)} %w_hbm.1) | copy-start | bytes 7962628
  3.7 1.0 copy-start.1
  4.6 1.0 copy-start.2

commit v2 on v1

v2 whole, which is shorter than its diff:
```python
import jax
import jax.numpy as jnp
import numpy as np
from jax import lax
from jax.experimental import pallas as pl
from jax.experimental.pallas import tpu as pltpu
from jax.sharding import PartitionSpec as P

MESH = pl.DeviceIdType.MESH
EPS = 1e-06
NC, NX, NY, NZ, NG = 2, 4, 8, 12, 6
ROWS, D = 128, 1152
OWN = 9
BLOCK = 144
COLS = 384
PARTS = 3
PIECE = 32
CHUNKS = 4
NT = COLS // 128
SLICE = ROWS // CHUNKS
HALF = ROWS // 2
F32, BF16 = jnp.float32, jnp.bfloat16


def dot(a, b, ca=1, cb=0):
    return lax.dot_general(a, b, (((ca,), (cb,)), ((), ())), preferred_element_type=F32)


def unit_rows(wide):
    inverse = lax.rsqrt(jnp.sum(wide * wide, axis=1, keepdims=True) + EPS)
    return wide * inverse, inverse


def kernel(
    mult_ref, bias_ref, a_hbm, t_hbm, w_hbm, order_hbm,
    head_ref, tgrad_ref,
    a_ref, t_ref, w_ref, order_ref, proj_ref, img_ref, tx, ix, relayed, igrad, tsum,
    at_all, at_got, p_got, out, pieces, ysend, ygot, zsend, zgot, final,
    local_sem, t_ss, t_rs, i_ss, i_rs, r_ss, r_rs, a_ss, a_rs,
    p_ss, p_rs, f_ss, q_ss, q_rs, y_ss, y_rs, z_ss, z_rs,
):
    b = lax.axis_index("blk")
    g = lax.axis_index("group")
    c, x, y, zh = b % 2, (b // 2) % NX, (b // 8) % NY, b // 64
    z = zh * NG + g

    def at(c_, x_, y_, z_):
        return ((z_ // NG) * 64 + y_ * 8 + x_ * 2 + c_, z_ % NG)

    after = ((b + 1) % 128, g)
    before = ((b + 127) % 128, g)
    up = (b, (g + 1) % NG)
    down = (b, (g + 5) % NG)
    partner = at(1 - c, x, y, z)
    right = at(c, (x + 1) % NX, y, z)
    left = at(c, (x + 3) % NX, y, z)

    far_z = (z + 6) % NZ
    is_source = (c == 1) & (x == 3) & (y == 7)
    is_target = (c == 0) & (x == 0) & (y == 0)
    is_relay = (c == 1) & (((x == 0) & (y == 7)) | ((x == 3) & (y == 0)) | ((x == 0) & (y == 0)))
    relay_chunk = jnp.where(y == 7, 1, jnp.where(x == 3, 2, 3))

    def relays_at(z_):
        return [None, at(1, 0, 7, z_), at(1, 3, 0, z_), at(1, 0, 0, z_)]

    loads = []
    for i, (src, dst) in enumerate(
        ((t_hbm, t_ref), (a_hbm, a_ref), (w_hbm, w_ref), (order_hbm, order_ref))
    ):
        load = pltpu.make_async_copy(src, dst, local_sem.at[i])
        load.start()
        loads.append(load)

    ring = [at(core, (x + k) % NX, y, z) for k in range(1, NX) for core in range(NC)]
    column = [at(c, x, (y + k) % NY, z) for k in range(1, NY)]
    tower = [at(c, x, y, (z + k) % NZ) for k in range(1, NZ)]
    greeted = [after, before, up, down, partner] + ring + column + tower
    barrier = pltpu.get_barrier_semaphore()

    def greet(device):
        pl.semaphore_signal(barrier, inc=1, device_id=device, device_id_type=MESH)

    for device in greeted:
        greet(device)

    @pl.when(is_source)
    def _():
        for device in relays_at(z)[1:]:
            greet(device)

    @pl.when(is_relay)
    def _():
        greet(at(1, 3, 7, z))
        greet(at(0, 0, 0, far_z))

    @pl.when(is_target)
    def _():
        for device in relays_at(far_z)[1:]:
            greet(device)

    loads[0].wait()
    ends = is_source.astype(jnp.int32) + is_target.astype(jnp.int32)
    pl.semaphore_wait(barrier, len(greeted) + 3 * ends + 2 * is_relay.astype(jnp.int32))

    started = []

    def remote(src, dst, ss, rs, device):
        return pltpu.make_async_remote_copy(
            src_ref=src, dst_ref=dst, send_sem=ss, recv_sem=rs, device_id=device, device_id_type=MESH
        )

    def send(src, dst, ss, rs, device):
        copy = remote(src, dst, ss, rs, device)
        copy.start()
        started.append(copy)
        return copy

    def chunk(k):
        return pl.ds(k * SLICE, SLICE)

    def send_after(src, dst, kind, ss, rs, k):
        direct = remote(src, dst, ss, rs, after)
        started.append(direct)
        if k == 0:
            direct.start()
        else:
            @pl.when(is_source)
            def _():
                remote(src, relayed.at[kind], ss, r_rs.at[kind], relays_at(z)[k]).start()

            @pl.when(jnp.logical_not(is_source))
            def _():
                direct.start()
        return direct

    def relay_copy(kind, dst, rs):
        piece = pl.ds(pl.multiple_of(relay_chunk * SLICE, SLICE), SLICE)
        return remote(
            relayed.at[kind], dst.at[piece], r_ss.at[kind], rs.at[relay_chunk], at(0, 0, 0, far_z)
        )

    def relay(kind, dst, rs):
        @pl.when(is_relay)
        def _():
            remote(relayed.at[kind], relayed.at[kind], r_ss.at[kind], r_rs.at[kind], after).wait_recv()
            relay_copy(kind, dst, rs).start()

    def relay_end(kind, dst, rs):
        @pl.when(is_relay)
        def _():
            relay_copy(kind, dst, rs).wait_send()

    def text_hop(hop, k, source):
        return (source.at[chunk(k)], tx.at[hop, chunk(k)], t_ss.at[hop, k], t_rs.at[hop, k])

    def image_hop(hop, k, source):
        return (source.at[chunk(k)], ix.at[hop, chunk(k)], i_ss.at[hop, k], i_rs.at[hop, k])

    def after_hop(args, kind, k):
        src, dst, ss, rs = args
        return send_after(src, dst, kind, ss, rs, k)

    hop1 = [after_hop(text_hop(0, k, t_ref), 0, k) for k in range(CHUNKS)]

    loads[1].wait()
    loads[2].wait()
    for k in range(3):
        cols = pl.ds(k * 384, 384)
        proj_ref[:, cols] = dot(a_ref[...], w_ref[:, cols])
    unit, img_inverse = unit_rows(proj_ref[...])
    img_ref[...] = unit.astype(BF16)
    i_hop1 = [after_hop(image_hop(0, k, img_ref), 1, k) for k in range(CHUNKS)]

    multiplier = mult_ref[0]
    bias = bias_ref[0]

    def txt_of(raw):
        return unit_rows(raw.astype(F32))[0].astype(BF16)

    rows = lax.broadcasted_iota(jnp.int32, (ROWS, ROWS), 0)
    cols = lax.broadcasted_iota(jnp.int32, (ROWS, ROWS), 1)
    positive = jnp.where(rows == cols, 1.0, 0.0).astype(F32)

    def scaled_of(left_rows, right_rows, own):
        logits = multiplier * dot(left_rows, right_rows, 1, 1) + bias
        weight = jax.nn.sigmoid(logits)
        if own:
            weight = weight - positive
        return (multiplier * weight).astype(BF16)

    def image_pair(raw, own):
        txt_b = txt_of(raw)
        term = dot(scaled_of(img_ref[...], txt_b, own), txt_b)
        if own:
            igrad[...] = term
        else:
            igrad[...] += term

    hop2 = []
    for k in range(CHUNKS):
        hop1[k].wait_recv()
        hop2.append(send(*text_hop(1, k, tx.at[0]), up))
    relay(0, tx.at[0], t_rs.at[0])
    loads[3].wait()
    for k in range(NX * NC):
        at_all[k] = dot(order_ref[pl.ds(k * BLOCK, BLOCK), :], a_ref[...], 1, 1).astype(BF16)
    at_got[0, :, :128] = at_all[x * 2 + c]
    a_copies = []
    for k in range(NX):
        for dc in range(NC):
            slot = k * 2 + dc
            if slot == 0:
                continue
            to_x, to_c = (x + k) % NX, (c + dc) % 2
            a_copies.append(
                send(
                    at_all.at[to_x * 2 + to_c], at_got.at[k, :, pl.ds(dc * 128, 128)],
                    a_ss.at[slot], a_rs.at[slot], at(to_c, to_x, y, z),
                )
            )
    image_pair(t_ref[...], True)
    image_pair(tx[0], False)
    for q in range(PARTS):
        for half in range(2):
            pieces[q, :, half * PIECE + NT * OWN : (half + 1) * PIECE, :] = jnp.zeros(
                (NY, PIECE - NT * OWN, 128), F32
            )
    relay(1, ix.at[0], i_rs.at[0])
    hop3 = []
    for k in range(CHUNKS):
        hop2[k].wait_recv()
        hop3.append(after_hop(text_hop(2, k, tx.at[1]), 2, k))
    relay(2, tx.at[2], t_rs.at[2])
    image_pair(tx[1], False)
    i_hop2 = []
    for k in range(CHUNKS):
        i_hop1[k].wait_recv()
        i_hop2.append(send(*image_hop(1, k, ix.at[0]), up))
    for k in range(CHUNKS):
        hop3[k].wait_recv()
    image_pair(tx[2], False)

    unit, img_inverse = unit_rows(proj_ref[...])
    grad = igrad[...]
    proj_grad = (
        (grad - unit * jnp.sum(unit * grad, axis=1, keepdims=True)) * img_inverse
    ).astype(BF16)
    for q in range(PARTS):
        p_got[0, q, :ROWS] = proj_grad[:, q * COLS : (q + 1) * COLS]

    first, second = pl.ds(0, HALF), pl.ds(HALF, HALF)
    own_rows, partner_rows = pl.ds(0, ROWS), pl.ds(ROWS, ROWS)
    p_copies, q_copies, f_copies, y_copies = {}, {}, {}, {}

    def p_send(k, q, half, device):
        rows_ = (first, second)[half]
        p_copies[k, q, half] = send(
            p_got.at[0, q, rows_], p_got.at[k, q, rows_], p_ss.at[k, q, half], p_rs.at[k, q, half], device
        )

    def q_send(k, q):
        q_copies[k, q] = send(
            p_got.at[k, q, own_rows], p_got.at[k, q, partner_rows], q_ss.at[k, q], q_rs.at[k, q], partner
        )

    for q in range(PARTS):
        p_send(1, q, 0, right)
        p_send(3, q, 1, left)
        p_send(1, q, 1, right)
        p_send(3, q, 0, left)
    for q in range(PARTS):
        q_send(0, q)

    def forward(q):
        p_copies[1, q, 0].wait_recv()
        f_copies[q, 0] = send(
            p_got.at[1, q, first], p_got.at[2, q, first], f_ss.at[q, 0], p_rs.at[2, q, 0], right
        )
        p_copies[3, q, 1].wait_recv()
        f_copies[q, 1] = send(
            p_got.at[3, q, second], p_got.at[2, q, second], f_ss.at[q, 1], p_rs.at[2, q, 1], left
        )

    def over_x(q):
        p_copies[1, q, 1].wait_recv()
        q_send(1, q)
        p_copies[3, q, 0].wait_recv()
        q_send(3, q)
        f_copies[q, 0].wait_recv()
        f_copies[q, 1].wait_recv()
        q_send(2, q)
        for k in range(NX):
            q_copies[k, q].wait_recv()
        acc = dot(at_got[0], p_got[0, q])
        for k in range(1, NX):
            acc = acc + dot(at_got[k], p_got[k, q])
        out[...] = acc
        for to_y in range(NY):
            for half in range(2):
                for j in range(NT):
                    source = (to_y * 2 + half) * OWN
                    target = half * PIECE + j * OWN
                    pieces[q, to_y, target : target + OWN, :] = out[
                        source : source + OWN, j * 128 : (j + 1) * 128
                    ]
        ysend[q] = pieces[q].astype(BF16)
        for k in (4, 3, 5, 2, 6, 1, 7):
            to_y = (y + k) % NY
            y_copies[q, k] = send(
                ysend.at[q, to_y], ygot.at[q, k], y_ss.at[q, k], y_rs.at[q, k], at(c, x, to_y, z)
            )

    z_copies = {}

    def over_y(q):
        total = pieces[q, y]
        for k in (1, 7, 2, 6, 3, 5, 4):
            y_copies[q, k].wait_recv()
            total = total + ygot[q, k].astype(F32)
        zsend[q, 0] = total[:PIECE].astype(BF16)
        zsend[q, 1] = total[PIECE:].astype(BF16)
        zgot[q, z] = zsend[q, zh]
        for k in (6, 5, 7, 4, 8, 3, 9, 2, 10, 1, 11):
            to_z = (z + k) % NZ
            z_copies[q, k] = send(
                zsend.at[q, to_z // NG], zgot.at[q, z], z_ss.at[q, k], z_rs.at[q, k], at(c, x, y, to_z)
            )

    for copy in a_copies:
        copy.wait_recv()
    forward(0)
    forward(1)
    over_x(0)
    forward(2)
    i_hop3 = []
    for k in range(CHUNKS):
        i_hop2[k].wait_recv()
        i_hop3.append(after_hop(image_hop(2, k, ix.at[1]), 3, k))
    over_x(1)
    relay(3, ix.at[2], i_rs.at[2])
    over_y(0)
    over_x(2)
    over_y(1)
    over_y(2)

    txt_b = txt_of(tx[2])

    def text_pair(image, own):
        return dot(scaled_of(txt_b, image, own), image)

    tsum[...] = text_pair(img_ref[...], False)
    tsum[...] += text_pair(ix[0], False)
    tsum[...] += text_pair(ix[1], False)

    for k in range(CHUNKS):
        i_hop3[k].wait_recv()
    tsum[...] += text_pair(ix[2], True)
    grad = tsum[...]
    unit_txt, txt_inverse = unit_rows(tx[2].astype(F32))
    tgrad_ref[...] = (
        (grad - unit_txt * jnp.sum(unit_txt * grad, axis=1, keepdims=True)) * txt_inverse
    ).astype(BF16)

    for q in range(PARTS):
        for k in (1, 11, 2, 10, 3, 9, 4, 8, 5, 7, 6):
            z_copies[q, k].wait_recv()
        total = zgot[q, 0].astype(F32)
        for k in range(1, NZ):
            total = total + zgot[q, k].astype(F32)
        final[...] = total
        for j in range(NT):
            target = (q * NT + j) * 128
            head_ref[:, target : target + 128] = final[j * OWN : (j + 1) * OWN, :].astype(BF16)

    for copy in started:
        copy.wait_send()
    relay_end(0, tx.at[0], t_rs.at[0])
    relay_end(1, ix.at[0], i_rs.at[0])
    relay_end(2, tx.at[2], t_rs.at[2])
    relay_end(3, ix.at[2], i_rs.at[2])


def row_order():
    source = np.arange(D).reshape(2, NY, NX, NC, OWN).transpose(2, 3, 1, 0, 4).reshape(-1)
    order = np.zeros((D, D), np.float32)
    order[np.arange(D), source] = 1.0
    return order


def local(descriptors, captions, weights, multiplier, bias):
    order = jnp.asarray(row_order(), BF16)
    vmem = pl.BlockSpec(memory_space=pltpu.VMEM)
    smem = pl.BlockSpec(memory_space=pltpu.SMEM)
    hbm = pl.BlockSpec(memory_space=pltpu.HBM)
    dma = pltpu.SemaphoreType.DMA
    head, text = pl.pallas_call(
        kernel,
        out_shape=(
            jax.ShapeDtypeStruct((OWN, D), BF16),
            jax.ShapeDtypeStruct((ROWS, D), BF16),
        ),
        in_specs=[smem, smem, hbm, hbm, hbm, hbm],
        out_specs=(vmem, vmem),
        scratch_shapes=[
            pltpu.VMEM((ROWS, D), BF16),
            pltpu.VMEM((ROWS, D), BF16),
            pltpu.VMEM((D, D), BF16),
            pltpu.VMEM((D, D), BF16),
            pltpu.VMEM((ROWS, D), F32),
            pltpu.VMEM((ROWS, D), BF16),
            pltpu.VMEM((3, ROWS, D), BF16),
            pltpu.VMEM((3, ROWS, D), BF16),
            pltpu.VMEM((4, SLICE, D), BF16),
            pltpu.VMEM((ROWS, D), F32),
            pltpu.VMEM((ROWS, D), F32),
            pltpu.VMEM((NX * NC, BLOCK, ROWS), BF16),
            pltpu.VMEM((NX, BLOCK, NC * ROWS), BF16),
            pltpu.VMEM((NX, PARTS, NC * ROWS, COLS), BF16),
            pltpu.VMEM((BLOCK, COLS), F32),
            pltpu.VMEM((PARTS, NY, 2 * PIECE, 128), F32),
            pltpu.VMEM((PARTS, NY, 2 * PIECE, 128), BF16),
            pltpu.VMEM((PARTS, NY, 2 * PIECE, 128), BF16),
            pltpu.VMEM((PARTS, 2, PIECE, 128), BF16),
            pltpu.VMEM((PARTS, NZ, PIECE, 128), BF16),
            pltpu.VMEM((PIECE, 128), F32),
            dma((4,)),
            dma((3, CHUNKS)),
            dma((3, CHUNKS)),
            dma((3, CHUNKS)),
            dma((3, CHUNKS)),
            dma((4,)),
            dma((4,)),
            dma((NX * NC,)),
            dma((NX * NC,)),
            dma((NX, PARTS, 2)),
            dma((NX, PARTS, 2)),
            dma((PARTS, 2)),
            dma((NX, PARTS)),
            dma((NX, PARTS)),
            dma((PARTS, NY)),
            dma((PARTS, NY)),
            dma((PARTS, NZ)),
            dma((PARTS, NZ)),
        ],
        compiler_params=pltpu.CompilerParams(
            collective_id=0, has_side_effects=True, vmem_limit_bytes=60 * 1024 * 1024
        ),
        name="window_grads",
    )(multiplier, bias, descriptors, captions, weights, order)
    return head, text


def solution(mesh):
    in_specs = (P(("blk", "group"), None), P(("blk", "group"), None), P(), P(), P())
    out_specs = (P("blk", None), P(("blk", "group"), None))
    return jax.shard_map(local, mesh=mesh, in_specs=in_specs, out_specs=out_specs, check_vma=False)
```

time: 103 us -> 84.1 us (0.82)
  the two profiles are of different devices: /device:TPU:64 before, /device:TPU:1 now
where the time goes in v2:
time: 84.1 us; the launch traced here: 83.9 us
  Pallas kernels  78.9 us (94%)
  local copies, waits for them, and re-layouts  3.08 us (4%)
  between operations  1.93 us (2%)
    pallas_call x1, Pallas kernels, local(): pl.pallas_call(kernel, out_shape=(jax.ShapeDtypeStruct((OWN, D), BF16), j...  78.9 us
    unnamed x2, local copies, waits for them, and re-layouts  3.08 us

profile of v2, /device:TPU:1, one launch (start us, length us, event | category | flops | bytes accessed | tf_op | source)
XLA Modules:
  0.0 83.9 jit_solution(16116201948966336006)
XLA Ops:
  1.9 78.9 %window_grads.1 = (bf16[9,1152]{1,0:T(8,128)(2,1)}, bf16[128,1152]{1,0:T(8,128)(2,1)}) custom-call(f32[1]{0:T(128)S(6)} %copy.10.mult_ref, f32[1]{0:T(128)S(6)} %copy.11.bias_ref, bf16[128,1152]{1,0:T(8,128)(2,1)} %a_hbm.1, bf16[128,1152]{1,0:T(8,128)(2,1)} %t_hbm.1, bf16[1152,1152]{1,0:T(8,128)(2,1)} %w_hbm.1, bf16[1152,1152]{1,0:T(8,128)(2,1)} %constant.2.clone.order_hbm), custom_call_target="tpu_custom_call" | custom-call | tf_op jit(solution)/shard_map/window_grads/pallas_call | solution.py:397
  80.8 1.4 %copy.12 = bf16[9,1152]{1,0:T(8,128)(2,1)} copy(bf16[9,1152]{1,0:T(8,128)(2,1)} %get-tuple-element.4) | data formatting | bytes 41472
  82.2 1.7 %copy.13 = bf16[128,1152]{1,0:T(8,128)(2,1)} copy(bf16[128,1152]{1,0:T(8,128)(2,1)} %get-tuple-element.5) | data formatting | bytes 589824

commit v3 on v2

--- a/solution.py
+++ b/solution.py
@@ -19,6 +19,8 @@
 NT = COLS // 128
 SLICE = ROWS // CHUNKS
 HALF = ROWS // 2
+RELAYS = ((0, 3, 7), (1, 0, 7), (1, 3, 0), (1, 0, 0), (1, 2, 7), (1, 2, 0), (1, 3, 6), (1, 0, 6))
+STRIP = ROWS // len(RELAYS)
 F32, BF16 = jnp.float32, jnp.bfloat16
 
 
@@ -36,7 +38,7 @@
     head_ref, tgrad_ref,
     a_ref, t_ref, w_ref, order_ref, proj_ref, img_ref, tx, ix, relayed, igrad, tsum,
     at_all, at_got, p_got, out, pieces, ysend, ygot, zsend, zgot, final,
-    local_sem, t_ss, t_rs, i_ss, i_rs, r_ss, r_rs, a_ss, a_rs,
+    near_y, mid_y, near_z, mid_z, far_sem, local_sem, s_ss, t_ss, t_rs, i_ss, i_rs, r_ss, r_rs, a_ss, a_rs,
     p_ss, p_rs, f_ss, q_ss, q_rs, y_ss, y_rs, z_ss, z_rs,
 ):
     b = lax.axis_index("blk")
@@ -58,11 +60,21 @@
     far_z = (z + 6) % NZ
     is_source = (c == 1) & (x == 3) & (y == 7)
     is_target = (c == 0) & (x == 0) & (y == 0)
-    is_relay = (c == 1) & (((x == 0) & (y == 7)) | ((x == 3) & (y == 0)) | ((x == 0) & (y == 0)))
-    relay_chunk = jnp.where(y == 7, 1, jnp.where(x == 3, 2, 3))
+    is_second = (c == 0) & (x == 3) & (y == 7)
+    place = (y * NX + x) * NC + c
+    is_third, relay_strip = b < 0, 0
+    for i, (c_, x_, y_) in enumerate(RELAYS):
+        here = place == (y_ * NX + x_) * NC + c_
+        if i:
+            is_third = is_third | here
+        relay_strip = relay_strip + i * here.astype(jnp.int32)
+    is_relay = is_second | is_third
+    other = (1 - zh) * NG
+    target_z = (far_z, other + (g + 1) % NG)
+    origin_z = (far_z, other + (g + 5) % NG)
 
     def relays_at(z_):
-        return [None, at(1, 0, 7, z_), at(1, 3, 0, z_), at(1, 0, 0, z_)]
+        return [at(*spot, z_) for spot in RELAYS]
 
     loads = []
     for i, (src, dst) in enumerate(
@@ -73,9 +85,9 @@
         loads.append(load)
 
     ring = [at(core, (x + k) % NX, y, z) for k in range(1, NX) for core in range(NC)]
-    column = [at(c, x, (y + k) % NY, z) for k in range(1, NY)]
-    tower = [at(c, x, y, (z + k) % NZ) for k in range(1, NZ)]
-    greeted = [after, before, up, down, partner] + ring + column + tower
+    column = [at(c, x, (y + k) % NY, z) for k in (1, 7)]
+    tower = [at(c, x, y, (z + k) % NZ) for k in (1, 11)]
+    greeted = [up, down, partner] + ring + column + tower
     barrier = pltpu.get_barrier_semaphore()
 
     def greet(device):
@@ -84,26 +96,46 @@
     for device in greeted:
         greet(device)
 
-    @pl.when(is_source)
+    @pl.when(jnp.logical_not(is_source))
     def _():
-        for device in relays_at(z)[1:]:
-            greet(device)
+        greet(after)
+
+    @pl.when(jnp.logical_not(is_target))
+    def _():
+        greet(before)
 
     @pl.when(is_relay)
     def _():
         greet(at(1, 3, 7, z))
-        greet(at(0, 0, 0, far_z))
+
+    @pl.when(is_third)
+    def _():
+        greet(at(0, 3, 7, z))
 
     @pl.when(is_target)
     def _():
-        for device in relays_at(far_z)[1:]:
-            greet(device)
+        for z_ in origin_z:
+            for device in relays_at(z_):
+                greet(device)
 
     loads[0].wait()
-    ends = is_source.astype(jnp.int32) + is_target.astype(jnp.int32)
-    pl.semaphore_wait(barrier, len(greeted) + 3 * ends + 2 * is_relay.astype(jnp.int32))
-
-    started = []
+    def one(flag):
+        return flag.astype(jnp.int32)
+
+    expected = len(greeted) + 2 + (len(RELAYS) - 1) * one(is_source) - one(is_target)
+    expected = expected + 2 * one(is_relay) + (len(RELAYS) - 1) * one(is_second)
+    pl.semaphore_wait(barrier, expected)
+
+    def tell(sem, devices):
+        for device in devices:
+            pl.semaphore_signal(sem, inc=1, device_id=device, device_id_type=MESH)
+
+    two_column = [at(c, x, (y + k) % NY, z) for k in (2, 6)]
+    two_tower = [at(c, x, y, (z + k) % NZ) for k in (2, 10)]
+    tell(near_y, column)
+    tell(near_z, tower)
+
+    started, kept = [], []
 
     def remote(src, dst, ss, rs, device):
         return pltpu.make_async_remote_copy(
@@ -116,35 +148,72 @@
         started.append(copy)
         return copy
 
+    def strip(i):
+        return pl.ds(i * STRIP, STRIP)
+
     def chunk(k):
         return pl.ds(k * SLICE, SLICE)
 
-    def send_after(src, dst, kind, ss, rs, k):
+    def send_after(src, dst, kind, ss, rs, k, whole):
         direct = remote(src, dst, ss, rs, after)
-        started.append(direct)
-        if k == 0:
-            direct.start()
+        if kind >= 2:
+            kept.append(direct)
         else:
+            started.append(direct)
+
             @pl.when(is_source)
             def _():
-                remote(src, relayed.at[kind], ss, r_rs.at[kind], relays_at(z)[k]).start()
-
-            @pl.when(jnp.logical_not(is_source))
+                for i in range(k * SLICE // STRIP, (k + 1) * SLICE // STRIP):
+                    remote(
+                        whole.at[strip(i)], relayed.at[kind], ss, r_rs.at[kind], relays_at(z)[i]
+                    ).start()
+
+        @pl.when(jnp.logical_not(is_source))
+        def _():
+            direct.start()
+
+        return direct
+
+    def second_copies(src, kind):
+        return [
+            remote(src.at[strip(i)], relayed.at[kind], s_ss.at[kind - 2, i], r_rs.at[kind], relays_at(z)[i])
+            for i in range(1, len(RELAYS))
+        ]
+
+    def second_start(src, kind):
+        @pl.when(is_second)
+        def _():
+            for copy in second_copies(src, kind):
+                copy.start()
+
+    def second_end(src, kind):
+        @pl.when(is_second)
+        def _():
+            for copy in second_copies(src, kind):
+                copy.wait_send()
+
+    def relay_copy(kind, dst, rs):
+        piece = pl.ds(pl.multiple_of(relay_strip * STRIP, STRIP), STRIP)
+        return remote(
+            relayed.at[kind], dst.at[piece], r_ss.at[kind], rs.at[relay_strip * STRIP // SLICE],
+            at(0, 0, 0, target_z[kind // 2]),
+        )
+
+    def relay_own(kind, src, dst, rs):
+        return remote(src.at[strip(0)], dst.at[strip(0)], r_ss.at[kind], rs.at[0], at(0, 0, 0, target_z[1]))
+
+    def relay(kind, dst, rs, when):
+        through = is_relay if kind < 2 else is_third
+
+        @pl.when(through & when)
+        def _():
+            remote(relayed.at[kind], relayed.at[kind], r_ss.at[kind], r_rs.at[kind], up).wait_recv()
+            relay_copy(kind, dst, rs).start()
+
+        if kind >= 2:
+            @pl.when(is_second & when)
             def _():
-                direct.start()
-        return direct
-
-    def relay_copy(kind, dst, rs):
-        piece = pl.ds(pl.multiple_of(relay_chunk * SLICE, SLICE), SLICE)
-        return remote(
-            relayed.at[kind], dst.at[piece], r_ss.at[kind], rs.at[relay_chunk], at(0, 0, 0, far_z)
-        )
-
-    def relay(kind, dst, rs):
-        @pl.when(is_relay)
-        def _():
-            remote(relayed.at[kind], relayed.at[kind], r_ss.at[kind], r_rs.at[kind], after).wait_recv()
-            relay_copy(kind, dst, rs).start()
+                relay_own(kind, t_ref if kind == 2 else img_ref, dst, rs).start()
 
     def relay_end(kind, dst, rs):
         @pl.when(is_relay)
@@ -159,9 +228,12 @@
 
     def after_hop(args, kind, k):
         src, dst, ss, rs = args
-        return send_after(src, dst, kind, ss, rs, k)
+        return send_after(src, dst, kind, ss, rs, k, (t_ref, img_ref)[kind % 2])
 
     hop1 = [after_hop(text_hop(0, k, t_ref), 0, k) for k in range(CHUNKS)]
+    second_start(t_ref, 2)
+    relay(0, tx.at[0], t_rs.at[0], zh == 0)
+    relay(2, tx.at[2], t_rs.at[2], zh == 0)
 
     loads[1].wait()
     loads[2].wait()
@@ -171,6 +243,9 @@
     unit, img_inverse = unit_rows(proj_ref[...])
     img_ref[...] = unit.astype(BF16)
     i_hop1 = [after_hop(image_hop(0, k, img_ref), 1, k) for k in range(CHUNKS)]
+    second_start(img_ref, 3)
+    relay(0, tx.at[0], t_rs.at[0], zh == 1)
+    relay(2, tx.at[2], t_rs.at[2], zh == 1)
 
     multiplier = mult_ref[0]
     bias = bias_ref[0]
@@ -201,7 +276,10 @@
     for k in range(CHUNKS):
         hop1[k].wait_recv()
         hop2.append(send(*text_hop(1, k, tx.at[0]), up))
-    relay(0, tx.at[0], t_rs.at[0])
+    pl.semaphore_wait(near_y, 2)
+    pl.semaphore_wait(near_z, 2)
+    tell(mid_y, two_column)
+    tell(mid_z, two_tower)
     loads[3].wait()
     for k in range(NX * NC):
         at_all[k] = dot(order_ref[pl.ds(k * BLOCK, BLOCK), :], a_ref[...], 1, 1).astype(BF16)
@@ -219,6 +297,8 @@
                     a_ss.at[slot], a_rs.at[slot], at(to_c, to_x, y, z),
                 )
             )
+    relay(1, ix.at[0], i_rs.at[0], c >= 0)
+    relay(3, ix.at[2], i_rs.at[2], c >= 0)
     image_pair(t_ref[...], True)
     image_pair(tx[0], False)
     for q in range(PARTS):
@@ -226,17 +306,14 @@
             pieces[q, :, half * PIECE + NT * OWN : (half + 1) * PIECE, :] = jnp.zeros(
                 (NY, PIECE - NT * OWN, 128), F32
             )
-    relay(1, ix.at[0], i_rs.at[0])
     hop3 = []
     for k in range(CHUNKS):
         hop2[k].wait_recv()
         hop3.append(after_hop(text_hop(2, k, tx.at[1]), 2, k))
-    relay(2, tx.at[2], t_rs.at[2])
+    pl.semaphore_wait(mid_y, 2)
+    pl.semaphore_wait(mid_z, 2)
+    tell(far_sem, two_tower)
     image_pair(tx[1], False)
-    i_hop2 = []
-    for k in range(CHUNKS):
-        i_hop1[k].wait_recv()
-        i_hop2.append(send(*image_hop(1, k, ix.at[0]), up))
     for k in range(CHUNKS):
         hop3[k].wait_recv()
     image_pair(tx[2], False)
@@ -331,14 +408,18 @@
         copy.wait_recv()
     forward(0)
     forward(1)
+    i_hop2 = []
+    for k in range(CHUNKS):
+        i_hop1[k].wait_recv()
+        i_hop2.append(send(*image_hop(1, k, ix.at[0]), up))
     over_x(0)
     forward(2)
+    over_x(1)
+    pl.semaphore_wait(far_sem, 2)
     i_hop3 = []
     for k in range(CHUNKS):
         i_hop2[k].wait_recv()
         i_hop3.append(after_hop(image_hop(2, k, ix.at[1]), 3, k))
-    over_x(1)
-    relay(3, ix.at[2], i_rs.at[2])
     over_y(0)
     over_x(2)
     over_y(1)
@@ -378,6 +459,14 @@
     relay_end(0, tx.at[0], t_rs.at[0])
     relay_end(1, ix.at[0], i_rs.at[0])
     relay_end(2, tx.at[2], t_rs.at[2])
+    second_end(t_ref, 2)
+    second_end(img_ref, 3)
+
+    @pl.when(jnp.logical_not(is_source))
+    def _():
+        for copy in kept:
+            copy.wait_send()
+
     relay_end(3, ix.at[2], i_rs.at[2])
 
 
@@ -411,7 +500,7 @@
             pltpu.VMEM((ROWS, D), BF16),
             pltpu.VMEM((3, ROWS, D), BF16),
             pltpu.VMEM((3, ROWS, D), BF16),
-            pltpu.VMEM((4, SLICE, D), BF16),
+            pltpu.VMEM((4, STRIP, D), BF16),
             pltpu.VMEM((ROWS, D), F32),
             pltpu.VMEM((ROWS, D), F32),
             pltpu.VMEM((NX * NC, BLOCK, ROWS), BF16),
@@ -424,7 +513,13 @@
             pltpu.VMEM((PARTS, 2, PIECE, 128), BF16),
             pltpu.VMEM((PARTS, NZ, PIECE, 128), BF16),
             pltpu.VMEM((PIECE, 128), F32),
+            pltpu.SemaphoreType.REGULAR,
+            pltpu.SemaphoreType.REGULAR,
+            pltpu.SemaphoreType.REGULAR,
+            pltpu.SemaphoreType.REGULAR,
+            pltpu.SemaphoreType.REGULAR,
             dma((4,)),
+            dma((2, len(RELAYS))),
             dma((3, CHUNKS)),
             dma((3, CHUNKS)),
             dma((3, CHUNKS)),

time: 84.1 us -> 77.1 us (0.917)
  Pallas kernels: 78.9 us -> 71.9 us
    pallas_call x1, Pallas kernels: 78.9 us -> 71.9 us  [local(): pl.pallas_call(kernel, out_shape=(jax.ShapeDtypeStruct((OWN, D), BF16), j...]
where the time goes in v3:
time: 77.1 us; the launch traced here: 76.9 us
  Pallas kernels  71.9 us (93%)
  local copies, waits for them, and re-layouts  3.08 us (4%)
  between operations  1.93 us (3%)
    pallas_call x1, Pallas kernels, local(): pl.pallas_call(kernel, out_shape=(jax.ShapeDtypeStruct((OWN, D), BF16), j...  71.9 us
    unnamed x2, local copies, waits for them, and re-layouts  3.08 us

profile of v3, /device:TPU:1, one launch (start us, length us, event | category | flops | bytes accessed | tf_op | source)
XLA Modules:
  0.0 76.9 jit_solution(7981509159389147335)
XLA Ops:
  1.9 71.9 %window_grads.1 = (bf16[9,1152]{1,0:T(8,128)(2,1)}, bf16[128,1152]{1,0:T(8,128)(2,1)}) custom-call(f32[1]{0:T(128)S(6)} %copy.10.mult_ref, f32[1]{0:T(128)S(6)} %copy.11.bias_ref, bf16[128,1152]{1,0:T(8,128)(2,1)} %a_hbm.1, bf16[128,1152]{1,0:T(8,128)(2,1)} %t_hbm.1, bf16[1152,1152]{1,0:T(8,128)(2,1)} %w_hbm.1, bf16[1152,1152]{1,0:T(8,128)(2,1)} %constant.2.clone.order_hbm), custom_call_target="tpu_custom_call" | custom-call | tf_op jit(solution)/shard_map/window_grads/pallas_call | solution.py:486
  73.8 1.4 %copy.12 = bf16[9,1152]{1,0:T(8,128)(2,1)} copy(bf16[9,1152]{1,0:T(8,128)(2,1)} %get-tuple-element.4) | data formatting | bytes 41472
  75.2 1.7 %copy.13 = bf16[128,1152]{1,0:T(8,128)(2,1)} copy(bf16[128,1152]{1,0:T(8,128)(2,1)} %get-tuple-element.5) | data formatting | bytes 589824

commit v4 on v3

--- a/solution.py
+++ b/solution.py
@@ -15,11 +15,12 @@
 COLS = 384
 PARTS = 3
 PIECE = 32
-CHUNKS = 4
+CHUNKS = 2
 NT = COLS // 128
 SLICE = ROWS // CHUNKS
 HALF = ROWS // 2
 RELAYS = ((0, 3, 7), (1, 0, 7), (1, 3, 0), (1, 0, 0), (1, 2, 7), (1, 2, 0), (1, 3, 6), (1, 0, 6))
+IMAGE_RELAYS = ((0, 3, 7), (1, 1, 7), (1, 1, 0), (1, 3, 1), (1, 0, 1), (1, 2, 6), (1, 2, 1), (1, 1, 6))
 STRIP = ROWS // len(RELAYS)
 F32, BF16 = jnp.float32, jnp.bfloat16
 
@@ -62,19 +63,23 @@
     is_target = (c == 0) & (x == 0) & (y == 0)
     is_second = (c == 0) & (x == 3) & (y == 7)
     place = (y * NX + x) * NC + c
-    is_third, relay_strip = b < 0, 0
-    for i, (c_, x_, y_) in enumerate(RELAYS):
-        here = place == (y_ * NX + x_) * NC + c_
-        if i:
-            is_third = is_third | here
-        relay_strip = relay_strip + i * here.astype(jnp.int32)
+    carries = []
+    for spots in (RELAYS, IMAGE_RELAYS):
+        third, number = b < 0, 0
+        for i, (c_, x_, y_) in enumerate(spots):
+            here = place == (y_ * NX + x_) * NC + c_
+            if i:
+                third = third | here
+            number = number + i * here.astype(jnp.int32)
+        carries.append((third, number))
+    is_third = carries[0][0] | carries[1][0]
     is_relay = is_second | is_third
     other = (1 - zh) * NG
     target_z = (far_z, other + (g + 1) % NG)
     origin_z = (far_z, other + (g + 5) % NG)
 
-    def relays_at(z_):
-        return [at(*spot, z_) for spot in RELAYS]
+    def relays_at(z_, kind):
+        return [at(*spot, z_) for spot in (RELAYS, IMAGE_RELAYS)[kind % 2]]
 
     loads = []
     for i, (src, dst) in enumerate(
@@ -115,15 +120,15 @@
     @pl.when(is_target)
     def _():
         for z_ in origin_z:
-            for device in relays_at(z_):
+            for device in relays_at(z_, 0) + relays_at(z_, 1)[1:]:
                 greet(device)
 
     loads[0].wait()
     def one(flag):
         return flag.astype(jnp.int32)
 
-    expected = len(greeted) + 2 + (len(RELAYS) - 1) * one(is_source) - one(is_target)
-    expected = expected + 2 * one(is_relay) + (len(RELAYS) - 1) * one(is_second)
+    expected = len(greeted) + 2 + 2 * (len(RELAYS) - 1) * one(is_source) - one(is_target)
+    expected = expected + 2 * one(is_relay) + 2 * (len(RELAYS) - 1) * one(is_second)
     pl.semaphore_wait(barrier, expected)
 
     def tell(sem, devices):
@@ -165,7 +170,7 @@
             def _():
                 for i in range(k * SLICE // STRIP, (k + 1) * SLICE // STRIP):
                     remote(
-                        whole.at[strip(i)], relayed.at[kind], ss, r_rs.at[kind], relays_at(z)[i]
+                        whole.at[strip(i)], relayed.at[kind], ss, r_rs.at[kind], relays_at(z, kind)[i]
                     ).start()
 
         @pl.when(jnp.logical_not(is_source))
@@ -176,7 +181,7 @@
 
     def second_copies(src, kind):
         return [
-            remote(src.at[strip(i)], relayed.at[kind], s_ss.at[kind - 2, i], r_rs.at[kind], relays_at(z)[i])
+            remote(src.at[strip(i)], relayed.at[kind], s_ss.at[kind - 2, i], r_rs.at[kind], relays_at(z, kind)[i])
             for i in range(1, len(RELAYS))
         ]
 
@@ -193,6 +198,7 @@
                 copy.wait_send()
 
     def relay_copy(kind, dst, rs):
+        relay_strip = carries[kind % 2][1]
         piece = pl.ds(pl.multiple_of(relay_strip * STRIP, STRIP), STRIP)
         return remote(
             relayed.at[kind], dst.at[piece], r_ss.at[kind], rs.at[relay_strip * STRIP // SLICE],
@@ -203,7 +209,8 @@
         return remote(src.at[strip(0)], dst.at[strip(0)], r_ss.at[kind], rs.at[0], at(0, 0, 0, target_z[1]))
 
     def relay(kind, dst, rs, when):
-        through = is_relay if kind < 2 else is_third
+        third = carries[kind % 2][0]
+        through = (is_second | third) if kind < 2 else third
 
         @pl.when(through & when)
         def _():
@@ -216,7 +223,7 @@
                 relay_own(kind, t_ref if kind == 2 else img_ref, dst, rs).start()
 
     def relay_end(kind, dst, rs):
-        @pl.when(is_relay)
+        @pl.when(is_second | carries[kind % 2][0])
         def _():
             relay_copy(kind, dst, rs).wait_send()
 
@@ -280,6 +287,10 @@
     pl.semaphore_wait(near_z, 2)
     tell(mid_y, two_column)
     tell(mid_z, two_tower)
+    relay(1, ix.at[0], i_rs.at[0], c >= 0)
+    relay(3, ix.at[2], i_rs.at[2], c >= 0)
+    image_pair(t_ref[...], True)
+    image_pair(tx[0], False)
     loads[3].wait()
     for k in range(NX * NC):
         at_all[k] = dot(order_ref[pl.ds(k * BLOCK, BLOCK), :], a_ref[...], 1, 1).astype(BF16)
@@ -297,10 +308,6 @@
                     a_ss.at[slot], a_rs.at[slot], at(to_c, to_x, y, z),
                 )
             )
-    relay(1, ix.at[0], i_rs.at[0], c >= 0)
-    relay(3, ix.at[2], i_rs.at[2], c >= 0)
-    image_pair(t_ref[...], True)
-    image_pair(tx[0], False)
     for q in range(PARTS):
         for half in range(2):
             pieces[q, :, half * PIECE + NT * OWN : (half + 1) * PIECE, :] = jnp.zeros(

time: 77.1 us -> 75.6 us (0.981); the launches traced: 76.9 us -> 74.3 us
  Pallas kernels: 71.9 us -> 69.3 us
    pallas_call x1, Pallas kernels: 71.9 us -> 69.3 us  [local(): pl.pallas_call(kernel, out_shape=(jax.ShapeDtypeStruct((OWN, D), BF16), j...]
where the time goes in v4:
time: 75.6 us; the launch traced here: 74.3 us
  Pallas kernels  69.3 us (92%)
  local copies, waits for them, and re-layouts  3.08 us (4%)
  between operations  1.93 us (3%)
    pallas_call x1, Pallas kernels, local(): pl.pallas_call(kernel, out_shape=(jax.ShapeDtypeStruct((OWN, D), BF16), j...  69.3 us
    unnamed x2, local copies, waits for them, and re-layouts  3.08 us

profile of v4, /device:TPU:1, one launch (start us, length us, event | category | flops | bytes accessed | tf_op | source)
XLA Modules:
  0.0 74.3 jit_solution(16444897381826588982)
XLA Ops:
  1.9 69.3 %window_grads.1 = (bf16[9,1152]{1,0:T(8,128)(2,1)}, bf16[128,1152]{1,0:T(8,128)(2,1)}) custom-call(f32[1]{0:T(128)S(6)} %copy.10.mult_ref, f32[1]{0:T(128)S(6)} %copy.11.bias_ref, bf16[128,1152]{1,0:T(8,128)(2,1)} %a_hbm.1, bf16[128,1152]{1,0:T(8,128)(2,1)} %t_hbm.1, bf16[1152,1152]{1,0:T(8,128)(2,1)} %w_hbm.1, bf16[1152,1152]{1,0:T(8,128)(2,1)} %constant.2.clone.order_hbm), custom_call_target="tpu_custom_call" | custom-call | tf_op jit(solution)/shard_map/window_grads/pallas_call | solution.py:493
  71.2 1.4 %copy.12 = bf16[9,1152]{1,0:T(8,128)(2,1)} copy(bf16[9,1152]{1,0:T(8,128)(2,1)} %get-tuple-element.4) | data formatting | bytes 41472
  72.6 1.7 %copy.13 = bf16[128,1152]{1,0:T(8,128)(2,1)} copy(bf16[128,1152]{1,0:T(8,128)(2,1)} %get-tuple-element.5) | data formatting | bytes 589824
